TPU v7x, 256 devices: a whole 4x4x8 slice. The times are simulated.
256 devices in a mesh: attn: 64 (over x, z, core), tp: 4 (over y).
Axes of the slice: x: 4, y: 4, z: 8, core: 2. Of those that a mesh axis runs over, the one named last changes fastest.
Arguments:
- lengths: int32 [32], replicated, may hold values from 1 to 4, 64 in all
- queries: bfloat16 [32768, 2560], P('attn', 'tp'), may hold values from -8 to 8
- key_vectors: bfloat16 [32768, 512], P('attn', 'tp'), may hold values from -8 to 8
- value_vectors: bfloat16 [32768, 512], P('attn', 'tp'), may hold values from -6 to 6
- out_weight: bfloat16 [2560, 5120], P('tp'), may hold values from -0.125 to 0.125
- grad_output: bfloat16 [32768, 5120], P(('attn', 'tp')), may hold values from -6 to 6
Outputs:
- layer_out: bfloat16 [32768, 5120], P(('attn', 'tp'))
- grad_queries: bfloat16 [32768, 2560], P('attn', 'tp')
- grad_keys: bfloat16 [32768, 512], P('attn', 'tp')
- grad_values: bfloat16 [32768, 512], P('attn', 'tp')
Inputs may be any that keep to these rules, and one draw needn't show every extreme that they name: Document d covers lengths[d] whole blocks of 512 tokens; the documents follow one another and fill all 64 blocks; the longest covers exactly 4 blocks.
All inputs are finite; a program needn't handle non-finite values.
Results may differ from a plain program's by a relative error of at most 0.019.
Values may be sent and summed in bfloat16 or wider, within the bound.
A program may use at most 64 MiB of HBM per device.

v0:
```python
import functools

import jax
import jax.numpy as jnp
from jax import lax
from jax.experimental import pallas as pl
from jax.experimental.pallas import tpu as pltpu
from jax.sharding import PartitionSpec as P

HD = 128
REACH = 4
GROUP = 5
N_TP = 4
PARTS = 8
A_CHUNKS, B_CHUNKS = 4, 2
CHUNKS = A_CHUNKS + B_CHUNKS
Z = 8
NEGATIVE = -1e30
SCALE = HD ** (-0.5)
LOG2E = 1.4426950408889634
MESH = pl.DeviceIdType.MESH
BF, F32 = jnp.bfloat16, jnp.float32


def dot(a, b):
    return jnp.dot(a, b, preferred_element_type=F32)


def dot_nt(a, b):
    return lax.dot_general(a, b, (((1,), (1,)), ((), ())), preferred_element_type=F32)


def kernel(
    n,
    docs,
    len_ref,
    q_ref,
    k_ref,
    v_ref,
    w_ref,
    go_ref,
    lo_ref,
    gq_ref,
    gk_ref,
    gv_ref,
    qh,
    qt,
    kb,
    vb,
    kt,
    vt,
    wm,
    wp,
    go,
    acc,
    stat_m,
    stat_l,
    ot,
    o_all,
    op,
    rs_send,
    rs_recv,
    lo_acc,
    lo_out,
    dot_own,
    dot_part,
    dot_other,
    dot_send,
    dot_recv,
    dt,
    dd,
    delta,
    dk_acc,
    dv_acc,
    dq_acc,
    dkv_send,
    dkv_recv,
    gq_out,
    gk_out,
    gv_out,
    tabs_ref,
    loc_sem,
    out_sem,
    send_sem,
    recv_sem,
):
    tok, width = q_ref.shape
    row = tok // N_TP
    two = 2 * row
    feat = go_ref.shape[1]
    me, y = lax.axis_index("attn"), lax.axis_index("tp")
    step_x = n // 4
    core = lax.rem(me, 2)
    x = me // step_x
    y_a = y + 1 - 2 * lax.rem(y, 2)
    y_b = N_TP - 1 - y
    perm = [y, y_b, y_a, N_TP - 1 - y_a]

    def at(shift):
        return (lax.rem(me + shift + n, n), y)

    dev_a, dev_b = (me, y_a), (me, y_b)
    x_up, x_down = at(step_x), at(-step_x)
    z = lax.rem(me // 2, Z)
    z_up = (me + (lax.rem(z + 1, Z) - z) * 2, y)
    z_down = (me + (lax.rem(z + Z - 1, Z) - z) * 2, y)
    sib = (me + 1 - 2 * core, y)

    def part_of(shift):
        return lax.rem(x + shift + 4, 4) * 2 + core

    partners = [at(1), at(-1)] + [dev_a, dev_b, x_up, x_down]
    partners += [z_up, z_down]
    barrier = pltpu.get_barrier_semaphore()
    for dev in partners:
        pl.semaphore_signal(barrier, inc=1, device_id=dev, device_id_type=MESH)

    def local(i, src, dst):
        c = pltpu.make_async_copy(src, dst, loc_sem.at[i])
        c.start()
        return c

    loc_k = local(0, k_ref, kb.at[0])
    loc_v = local(1, v_ref, vb.at[0])
    loc_q = []
    for s in range(N_TP):
        rows = pl.ds(pl.multiple_of(perm[s] * row, row), row)
        for h in range(GROUP):
            loc_q.append(
                local(
                    2 + s * GROUP + h,
                    q_ref.at[rows, pl.ds(h * HD, HD)],
                    qh.at[h, pl.ds(s * row, row)],
                )
            )
    loc_go = local(2 + N_TP * GROUP, go_ref, go.at[0])
    loc_w = local(3 + N_TP * GROUP, w_ref, wm)

    pl.semaphore_wait(barrier, len(partners))

    used = [0]

    def remote(src, dst, dev):
        i = used[0]
        used[0] += 1
        c = pltpu.make_async_remote_copy(
            src_ref=src,
            dst_ref=dst,
            send_sem=send_sem.at[i],
            recv_sem=recv_sem.at[i],
            device_id=dev,
            device_id_type=MESH,
        )
        c.start()
        return c

    z_base = feat * 3 // 5
    wide = [z_base // A_CHUNKS] * A_CHUNKS + [(feat - z_base) // B_CHUNKS] * B_CHUNKS
    cols = [pl.ds(sum(wide[:j]), wide[j]) for j in range(CHUNKS)]
    side = [0] * A_CHUNKS + [1] * B_CHUNKS
    mine, from_down, from_up, from_far = [part_of(s) for s in (0, -1, 1, 2)]
    kv = [None, (remote(k_ref, kb.at[1], at(1)), remote(v_ref, vb.at[1], at(1)))]
    rows_of = [(dev_b, dev_a)[i] for i in side]
    wa, go_in = {}, {}

    def ask_weights(j):
        part = w_ref.at[mine, :, cols[j]]
        wa[j] = remote(part, wp.at[mine, :, cols[j]], dev_a)

    def ask_rows(j):
        go_in[j] = remote(go_ref.at[:, cols[j]], go.at[1, :, cols[j]], rows_of[j])

    z_wide = (feat - z_base) // Z

    def z_piece(ref, shift, low=0, many=PARTS // 2):
        first_col = pl.multiple_of(z_base + lax.rem(z + shift + Z, Z) * z_wide, z_wide)
        return ref.at[pl.ds(core * (PARTS // 2) + low, many), :, pl.ds(first_col, z_wide)]

    ask_weights(0)
    wb = remote(z_piece(w_ref, 0), z_piece(wp, 0), dev_b)
    ask_weights(1)
    ask_rows(0)
    ask_weights(2)
    ask_weights(3)
    ask_rows(1)
    ask_rows(4)
    ask_rows(2)
    ask_rows(5)
    ask_rows(3)

    z_sibs, z_ups, z_downs = [], [], []

    def z_share(piece):
        z_sibs.append(remote(piece, piece, sib))

    def z_first():
        wb.wait_recv()
        piece = z_piece(wp, 0)
        z_ups.append(remote(piece, piece, z_up))
        z_downs.append(remote(piece, piece, z_down))
        z_share(piece)

    def z_next(hop):
        last = hop == Z // 2 - 1
        z_ups[-1].wait_recv()
        piece = z_piece(wp, -hop)
        part = z_piece(wp, -hop, 0, PARTS // 4) if last else piece
        z_ups.append(remote(part, part, z_up))
        z_share(piece)
        z_downs[-1].wait_recv()
        piece = z_piece(wp, hop)
        part = z_piece(wp, hop, PARTS // 4, PARTS // 4) if last else piece
        z_downs.append(remote(part, part, z_down))
        z_share(piece)

    def z_last():
        z_ups[-1].wait_recv()
        z_share(z_piece(wp, Z // 2, 0, PARTS // 4))
        z_downs[-1].wait_recv()
        z_share(z_piece(wp, Z // 2, PARTS // 4, PARTS // 4))

    up, down, far = {}, {}, {}
    sibs = [[] for _ in range(A_CHUNKS)]

    def pass_own(j):
        wa[j].wait_recv()
        piece = wp.at[mine, :, cols[j]]
        up[j] = remote(piece, piece, x_up)
        down[j] = remote(piece, piece, x_down)
        sibs[j].append(remote(piece, piece, sib))

    def pass_near(j):
        up[j].wait_recv()
        piece = wp.at[from_down, :, cols[j]]
        if j % 2 == 0:
            far[j] = remote(piece, piece, x_up)
        sibs[j].append(remote(piece, piece, sib))
        down[j].wait_recv()
        piece = wp.at[from_up, :, cols[j]]
        if j % 2 == 1:
            far[j] = remote(piece, piece, x_down)
        sibs[j].append(remote(piece, piece, sib))

    def pass_far(j):
        far[j].wait_recv()
        piece = wp.at[from_far, :, cols[j]]
        sibs[j].append(remote(piece, piece, sib))

    def have(j):
        for c in sibs[j]:
            c.wait_recv()

    def next_keys(o):
        for c in kv[o]:
            c.wait_recv()
        if o < REACH - 1:
            kv.append(
                (
                    remote(kb.at[o], kb.at[o + 1], at(1)),
                    remote(vb.at[o], vb.at[o + 1], at(1)),
                )
            )

    end, first = jnp.int32(0), jnp.int32(0)
    for d in range(docs):
        end = end + len_ref[d]
        first = jnp.where(end <= me, end, first)
    depth = me - first

    def bias(o):
        return jnp.where(o <= depth, 0.0, -NEGATIVE).astype(F32)


    lane = lax.broadcasted_iota(jnp.int32, (1, row), 1)
    for s in range(N_TP):
        tabs_ref[:, s * row : (s + 1) * row] = lane + perm[s] * row

    c2 = SCALE * LOG2E

    for c in loc_q:
        c.wait()

    def turn_q(h, carry):
        qt[h] = qh[h].T
        return carry

    lax.fori_loop(0, GROUP, turn_q, 0)

    def turn_kv(o):
        kt[o] = kb[o].T
        vt[o] = vb[o].T

    def forward(o):
        turn_kv(o)

        def head(h, carry):
            s = dot(kb[o], qt[h])
            if o == 0:
                at_u = lax.broadcasted_iota(jnp.int32, (tok, tok), 0)
                s = jnp.where(at_u <= tabs_ref[...], s, NEGATIVE)
                new = jnp.max(s, axis=0, keepdims=True)
                p = jnp.exp2((s - new) * c2)
                stat_l[h] = jnp.sum(p, axis=0, keepdims=True)
                acc[h] = dot(vt[o], p.astype(BF))
            else:
                old = stat_m[h]
                new = jnp.maximum(old, jnp.max(s, axis=0, keepdims=True) - bias(o))
                fade = jnp.exp2((old - new) * c2)
                p = jnp.exp2((s - (new + bias(o))) * c2)
                stat_l[h] = stat_l[h] * fade + jnp.sum(p, axis=0, keepdims=True)
                acc[h] = acc[h] * fade + dot(vt[o], p.astype(BF))
            stat_m[h] = new

        for h in range(GROUP):
            head(h, None)

    loc_k.wait()
    loc_v.wait()
    forward(0)
    next_keys(1)
    z_first()
    pass_own(0)
    forward(1)
    pass_own(1)
    next_keys(2)
    forward(2)
    pass_own(2)
    z_next(1)
    next_keys(3)
    forward(3)
    pass_own(3)

    for h in range(GROUP):
        low = (acc[h] * (1.0 / stat_l[h])).astype(BF)
        ot[h] = low
        o_all[:, h * HD : (h + 1) * HD] = low.T
        stat_l[h] = stat_m[h] * c2 + jnp.log2(stat_l[h])
    o_in = [
        remote(o_all.at[pl.ds(two, two)], op.at[0], dev_a),
        remote(o_all.at[pl.ds(row, row)], op.at[1, pl.ds(0, row)], dev_b),
        remote(o_all.at[pl.ds(3 * row, row)], op.at[1, pl.ds(row, row)], dev_b),
    ]
    def weights(w3, j):
        return w3[:, :, cols[j]].reshape(width, wide[j])

    def add_to(total, part, fresh):
        if fresh:
            total[...] = part
        else:
            total[...] += part

    def cotangent_own():
        for j in range(CHUNKS):
            add_to(dot_own, dot_nt(weights(wm, j), go[0, :, cols[j]]), j == 0)

    def cotangent_rows(j):
        fresh = j in (0, A_CHUNKS)
        add_to(dot_part.at[side[j]], dot_nt(weights(wm, j), go[1, :, cols[j]]), fresh)

    def cotangent_other(j):
        both = go[:, :, cols[j]].reshape(two, wide[j])
        add_to(dot_other.at[side[j]], dot_nt(weights(wp, j), both), j in (0, A_CHUNKS))

    def send_cotangent(i):
        for h in range(GROUP):
            dot_send[i, h] = dot_other[i, h * HD : (h + 1) * HD, :].astype(BF)
        return remote(dot_send.at[i], dot_recv.at[i], [dev_a, dev_b][i])

    rs = {}

    def project(j):
        if side[j] == 0:
            mine_o, other_o = o_all[0:two], op[0]
        else:
            mine_o = jnp.concatenate([o_all[0:row], o_all[two : two + row]], axis=0)
            other_o = op[1]
        one = dot(mine_o, weights(wm, j)).astype(BF)
        other = dot(other_o, weights(wp, j)).astype(BF)
        both = one.astype(F32) + other.astype(F32)
        lo_acc[:, cols[j]] = both[0:row]
        rs_send[:, cols[j]] = both[row:two].astype(BF)

    def send_rows(j):
        rs[j] = remote(rs_send.at[:, cols[j]], rs_recv.at[:, cols[j]], rows_of[j])

    def turn_d(h, base, size, high):
        dt[h, :, base : base + size] = high
        dd[h, base : base + size] = high.T
        delta[h, :, base : base + size] = jnp.sum(
            high.astype(F32) * ot[h, :, base : base + size].astype(F32), axis=0, keepdims=True
        )

    def turn_own():
        for h in range(GROUP):
            turn_d(h, 0, row, dot_own[h * HD : (h + 1) * HD, :].astype(BF))

    def turn_rest():
        for h in range(GROUP):
            at_h = slice(h * HD, (h + 1) * HD)
            from_a, from_b = dot_recv[0, h].astype(F32), dot_recv[1, h].astype(F32)
            turn_d(h, row, row, (dot_part[0, at_h] + from_b[:, 0:row]).astype(BF))
            turn_d(h, two, row, (dot_part[1, at_h] + from_a[:, 0:row]).astype(BF))
            turn_d(h, 3 * row, row, (from_a[:, row:two] + from_b[:, row:two]).astype(BF))

    def backward(o, base, size):
        tl = slice(base, base + size)
        out = bias(o)

        def head(h):
            s = dot(kb[o], qt[h, :, tl])
            p = jnp.exp2(s * c2 - (stat_l[h, :, tl] + out))
            if base == 0 or (isinstance(o, int) and o == 0):
                at_u = lax.broadcasted_iota(jnp.int32, (tok, size), 0)
                p = jnp.where(at_u <= tabs_ref[:, tl] + jnp.where(o > 0, tok, 0), p, 0.0)
            dp = dot(vb[o], dt[h, :, tl])
            ds = (p * (dp - delta[h, :, tl])).astype(BF)
            part_v, part_k = dot(p.astype(BF), dd[h, tl]), dot(ds, qh[h, tl])
            if base == 0 and h == 0:
                dv_acc[o] = part_v
                dk_acc[o] = part_k
            else:
                dv_acc[o] += part_v
                dk_acc[o] += part_k
            dq_acc[h, :, tl] += dot(kt[o], ds)

        for h in range(GROUP):
            head(h)

    def own_rows(i, carry):
        backward(REACH - 1 - i, 0, row)
        return carry

    dq_acc[...] = jnp.zeros_like(dq_acc)
    dkv_recv[REACH - 1] = jnp.zeros((tok, 2 * HD), BF)

    pass_near(0)
    pass_near(1)
    loc_w.wait()
    loc_go.wait()
    cotangent_own()
    turn_own()
    z_next(2)
    lax.fori_loop(0, 2, own_rows, 0)
    pass_near(2)
    pass_near(3)
    for j in (0, 1):
        go_in[j].wait_recv()
        cotangent_rows(j)
    z_next(3)
    for j in (2, 3, 4, 5):
        go_in[j].wait_recv()
        cotangent_rows(j)
    for j in range(A_CHUNKS):
        pass_far(j)
    z_last()
    for j in range(A_CHUNKS):
        have(j)
        cotangent_other(j)
    d_in = [send_cotangent(0)]
    for c in z_sibs:
        c.wait_recv()
    cotangent_other(4)
    cotangent_other(5)
    d_in.append(send_cotangent(1))
    o_in[0].wait_recv()
    for j in (0, 1):
        project(j)
        send_rows(j)
    o_in[1].wait_recv()
    o_in[2].wait_recv()
    for j in (4, 2, 5, 3):
        project(j)
        send_rows(j)
    lax.fori_loop(2, REACH, own_rows, 0)
    for c in d_in:
        c.wait_recv()
    turn_rest()

    back_at = used[0]

    def back_copy(o):
        i = back_at + o
        c = pltpu.make_async_remote_copy(
            src_ref=dkv_send.at[o - 1],
            dst_ref=dkv_recv.at[o - 1],
            send_sem=send_sem.at[i],
            recv_sem=recv_sem.at[i],
            device_id=at(-1),
            device_id_type=MESH,
        )
        return c

    def sums(o):
        gk = dk_acc[o] * SCALE + dkv_recv[o, :, 0:HD].astype(F32)
        gv = dv_acc[o] + dkv_recv[o, :, HD : 2 * HD].astype(F32)
        return gk.astype(BF), gv.astype(BF)

    def other_rows(i, carry):
        o = REACH - 1 - i
        backward(o, row, tok - row)

        @pl.when(o < REACH - 1)
        def _():
            back_copy(o + 1).wait_recv()

        gk, gv = sums(o)
        dkv_send[o - 1, :, 0:HD] = gk
        dkv_send[o - 1, :, HD : 2 * HD] = gv
        back_copy(o).start()
        return carry

    lax.fori_loop(0, REACH - 1, other_rows, 0)
    backward(0, row, tok - row)

    outs = []

    def put(src, dst):
        c = pltpu.make_async_copy(src, dst, out_sem.at[len(outs)])
        c.start()
        outs.append(c)

    for h in range(GROUP):
        gq_out[:, h * HD : (h + 1) * HD] = (dq_acc[h] * SCALE).T.astype(BF)
    for s in range(N_TP):
        rows = pl.ds(pl.multiple_of(perm[s] * row, row), row)
        put(gq_out.at[pl.ds(s * row, row)], gq_ref.at[rows])

    for j in range(CHUNKS):
        rs[j].wait_recv()
        lo_out[:, cols[j]] = (lo_acc[:, cols[j]] + rs_recv[:, cols[j]].astype(F32)).astype(BF)
        put(lo_out.at[:, cols[j]], lo_ref.at[:, cols[j]])

    back_copy(1).wait_recv()
    gk_out[...], gv_out[...] = sums(0)
    put(gk_out, gk_ref)
    put(gv_out, gv_ref)

    sent = [c for pair in kv[1:] for c in pair] + o_in + d_in
    sent += [back_copy(o) for o in range(1, REACH)]
    sent += [wb] + z_sibs + z_ups + z_downs
    for j in range(CHUNKS):
        sent += [go_in[j], rs[j]]
    for j in range(A_CHUNKS):
        sent += [wa[j], up[j], down[j], far[j]] + sibs[j]
    for c in sent:
        c.wait_send()
    for c in outs:
        c.wait()


def settle(*refs):
    many = len(refs) // 3
    came, went, held, sems = refs[:many], refs[many : 2 * many], refs[2 * many : -1], refs[-1]
    loads = [pltpu.make_async_copy(came[i], held[i], sems.at[0, i]) for i in range(many)]
    stores = [pltpu.make_async_copy(held[i], went[i], sems.at[1, i]) for i in range(many)]
    for c in loads:
        c.start()
    for load, store in zip(loads, stores):
        load.wait()
        store.start()
    for c in stores:
        c.wait()


def on_device(n, lengths, queries, key_vectors, value_vectors, out_weight, grad_output):
    tok, width = queries.shape
    feat = out_weight.shape[1]
    row, two = tok // N_TP, tok // 2
    docs = lengths.shape[0]
    hbm = pl.BlockSpec(memory_space=pl.ANY)
    vm = pltpu.VMEM
    dma = pltpu.SemaphoreType.DMA
    flops = 2 * tok * width * feat * 2 + 7 * 2 * tok * tok * width * REACH
    found = pl.pallas_call(
        functools.partial(kernel, n, docs),
        out_shape=(
            jax.ShapeDtypeStruct((row, feat), BF),
            jax.ShapeDtypeStruct((tok, width), BF),
            jax.ShapeDtypeStruct((tok, HD), BF),
            jax.ShapeDtypeStruct((tok, HD), BF),
        ),
        in_specs=[pl.BlockSpec(memory_space=pltpu.SMEM)] + [hbm] * 5,
        out_specs=(hbm,) * 4,
        scratch_shapes=[
            vm((GROUP, tok, HD), BF),
            vm((GROUP, HD, tok), BF),
            vm((REACH, tok, HD), BF),
            vm((REACH, tok, HD), BF),
            vm((REACH, HD, tok), BF),
            vm((REACH, HD, tok), BF),
            vm((PARTS, width // PARTS, feat), BF),
            vm((PARTS, width // PARTS, feat), BF),
            vm((2, row, feat), BF),
            vm((GROUP, HD, tok), F32),
            vm((GROUP, 1, tok), F32),
            vm((GROUP, 1, tok), F32),
            vm((GROUP, HD, tok), BF),
            vm((tok, width), BF),
            vm((2, two, width), BF),
            vm((row, feat), BF),
            vm((row, feat), BF),
            vm((row, feat), F32),
            vm((row, feat), BF),
            vm((width, row), F32),
            vm((2, width, row), F32),
            vm((2, width, two), F32),
            vm((2, GROUP, HD, two), BF),
            vm((2, GROUP, HD, two), BF),
            vm((GROUP, HD, tok), BF),
            vm((GROUP, tok, HD), BF),
            vm((GROUP, 1, tok), F32),
            vm((REACH, tok, HD), F32),
            vm((REACH, tok, HD), F32),
            vm((GROUP, HD, tok), F32),
            vm((REACH - 1, tok, 2 * HD), BF),
            vm((REACH, tok, 2 * HD), BF),
            vm((tok, width), BF),
            vm((tok, HD), BF),
            vm((tok, HD), BF),
            vm((1, tok), jnp.int32),
            dma((4 + N_TP * GROUP,)),
            dma((16,)),
            dma((96,)),
            dma((96,)),
        ],
        compiler_params=pltpu.CompilerParams(
            collective_id=0, has_side_effects=True, vmem_limit_bytes=56 * 1024 * 1024
        ),
        cost_estimate=pl.CostEstimate(flops=flops, bytes_accessed=1 << 24, transcendentals=1 << 23),
    )(
        lengths,
        queries,
        key_vectors,
        value_vectors,
        out_weight.reshape(PARTS, width // PARTS, feat),
        grad_output,
    )
    return pl.pallas_call(
        settle,
        out_shape=tuple(jax.ShapeDtypeStruct(a.shape, a.dtype) for a in found),
        in_specs=[hbm] * 4,
        out_specs=(hbm,) * 4,
        scratch_shapes=[vm(a.shape, a.dtype) for a in found] + [dma((2, 4))],
    )(*found)


def solution(mesh):
    return jax.shard_map(
        functools.partial(on_device, mesh.shape["attn"]),
        mesh=mesh,
        in_specs=(
            P(),
            P("attn", "tp"),
            P("attn", "tp"),
            P("attn", "tp"),
            P("tp", None),
            P(("attn", "tp"), None),
        ),
        out_specs=(P(("attn", "tp"), None), P("attn", "tp"), P("attn", "tp"), P("attn", "tp")),
        check_vma=False,
    )
```

profile of v0, /device:TPU:1, one launch (start us, length us, event | category | flops | bytes accessed | tf_op | source)
XLA Modules:
  0.0 75.3 jit_solution(5034055801910637275)
XLA Ops:
  0.6 71.7 %shard_map.93 = (bf16[128,5120]{1,0:T(8,128)(2,1)}, bf16[512,640]{1,0:T(8,128)(2,1)}, bf16[512,128]{1,0:T(8,128)(2,1)}, bf16[512,128]{1,0:T(8,128)(2,1)}) custom-call(s32[32]{0:T(128)} %len_ref.1, bf16[512,640]{1,0:T(8,128)(2,1)} %q_ref.1, bf16[512,128]{1,0:T(8,128)(2,1)} %k_ref.1, bf16[512,128]{1,0:T(8,128)(2,1)} %v_ref.1, bf16[8,80,5120]{2,1,0:T(8,128)(2,1)} %bitcast.1, ...), custom_call_target="tpu_custom_call" | custom-call | flops 16106127360 | bytes 16777216 | tf_op jit(solution)/shard_map/pallas_call | solution.py:574
  72.4 2.7 %shard_map.94 = (bf16[128,5120]{1,0:T(8,128)(2,1)}, bf16[512,640]{1,0:T(8,128)(2,1)}, bf16[512,128]{1,0:T(8,128)(2,1)}, bf16[512,128]{1,0:T(8,128)(2,1)}) custom-call(bf16[128,5120]{1,0:T(8,128)(2,1)} %get-tuple-element.8.refs_0_, bf16[512,640]{1,0:T(8,128)(2,1)} %get-tuple-element.9.refs_1_, bf16[512,128]{1,0:T(8,128)(2,1)} %get-tuple-element.10.refs_2_, ...), custom_call_target="tpu_custom_call" | custom-call | tf_op jit(solution)/shard_map/pallas_call | solution.py:638
where the time goes:
time: 75.4 us; the launch traced here: 75.3 us
  Pallas kernels  74.5 us (99%)
  between operations  0.82 us (1%)
    pallas_call x1, Pallas kernels, on_device(): pl.pallas_call(functools.partial(kernel, n, docs), out_shape=(jax.ShapeDt...  71.7 us
    pallas_call x1, Pallas kernels, on_device(): pl.pallas_call(settle, out_shape=tuple((jax.ShapeDtypeStruct(a.shape, a.d...  2.73 us

commit v1 on v0

--- a/solution.py
+++ b/solution.py
@@ -20,6 +20,18 @@
 LOG2E = 1.4426950408889634
 MESH = pl.DeviceIdType.MESH
 BF, F32 = jnp.bfloat16, jnp.float32
+
+
+def span_of(h):
+    return pl.ds(pl.multiple_of(h * HD, HD), HD)
+
+
+def each_head(body):
+    def step(h, carry):
+        body(h)
+        return carry
+
+    lax.fori_loop(0, GROUP, step, 0)
 
 
 def dot(a, b):
@@ -61,7 +73,6 @@
     rs_send,
     rs_recv,
     lo_acc,
-    lo_out,
     dot_own,
     dot_part,
     dot_other,
@@ -75,12 +86,8 @@
     dq_acc,
     dkv_send,
     dkv_recv,
-    gq_out,
-    gk_out,
-    gv_out,
     tabs_ref,
     loc_sem,
-    out_sem,
     send_sem,
     recv_sem,
 ):
@@ -154,8 +161,10 @@
         c.start()
         return c
 
-    z_base = feat * 3 // 5
-    wide = [z_base // A_CHUNKS] * A_CHUNKS + [(feat - z_base) // B_CHUNKS] * B_CHUNKS
+    z_base = feat * 11 // 20
+    tiles = z_base // 128
+    wide = [(tiles + i) // A_CHUNKS * 128 for i in range(A_CHUNKS - 1, -1, -1)]
+    wide += [(feat - z_base) // B_CHUNKS] * B_CHUNKS
     cols = [pl.ds(sum(wide[:j]), wide[j]) for j in range(CHUNKS)]
     side = [0] * A_CHUNKS + [1] * B_CHUNKS
     mine, from_down, from_up, from_far = [part_of(s) for s in (0, -1, 1, 2)]
@@ -170,11 +179,12 @@
     def ask_rows(j):
         go_in[j] = remote(go_ref.at[:, cols[j]], go.at[1, :, cols[j]], rows_of[j])
 
-    z_wide = (feat - z_base) // Z
-
-    def z_piece(ref, shift, low=0, many=PARTS // 2):
-        first_col = pl.multiple_of(z_base + lax.rem(z + shift + Z, Z) * z_wide, z_wide)
-        return ref.at[pl.ds(core * (PARTS // 2) + low, many), :, pl.ds(first_col, z_wide)]
+    z_wide = (feat - z_base) // 2
+    z_half = (z_wide + 128) // 256 * 128
+
+    def z_piece(ref, shift, low=0, many=z_wide):
+        first_col = pl.multiple_of(z_base + core * z_wide + low, 128)
+        return ref.at[lax.rem(z + shift + Z, Z), :, pl.ds(first_col, many)]
 
     ask_weights(0)
     wb = remote(z_piece(w_ref, 0), z_piece(wp, 0), dev_b)
@@ -204,20 +214,20 @@
         last = hop == Z // 2 - 1
         z_ups[-1].wait_recv()
         piece = z_piece(wp, -hop)
-        part = z_piece(wp, -hop, 0, PARTS // 4) if last else piece
+        part = z_piece(wp, -hop, 0, z_half) if last else piece
         z_ups.append(remote(part, part, z_up))
         z_share(piece)
         z_downs[-1].wait_recv()
         piece = z_piece(wp, hop)
-        part = z_piece(wp, hop, PARTS // 4, PARTS // 4) if last else piece
+        part = z_piece(wp, hop, z_half, z_wide - z_half) if last else piece
         z_downs.append(remote(part, part, z_down))
         z_share(piece)
 
     def z_last():
         z_ups[-1].wait_recv()
-        z_share(z_piece(wp, Z // 2, 0, PARTS // 4))
+        z_share(z_piece(wp, Z // 2, 0, z_half))
         z_downs[-1].wait_recv()
-        z_share(z_piece(wp, Z // 2, PARTS // 4, PARTS // 4))
+        z_share(z_piece(wp, Z // 2, z_half, z_wide - z_half))
 
     up, down, far = {}, {}, {}
     sibs = [[] for _ in range(A_CHUNKS)]
@@ -310,9 +320,9 @@
                 stat_l[h] = stat_l[h] * fade + jnp.sum(p, axis=0, keepdims=True)
                 acc[h] = acc[h] * fade + dot(vt[o], p.astype(BF))
             stat_m[h] = new
-
-        for h in range(GROUP):
-            head(h, None)
+            return carry
+
+        lax.fori_loop(0, GROUP, head, 0, unroll=o > 0)
 
     loc_k.wait()
     loc_v.wait()
@@ -330,11 +340,13 @@
     forward(3)
     pass_own(3)
 
-    for h in range(GROUP):
+    def finish(h):
         low = (acc[h] * (1.0 / stat_l[h])).astype(BF)
         ot[h] = low
-        o_all[:, h * HD : (h + 1) * HD] = low.T
+        o_all[:, span_of(h)] = low.T
         stat_l[h] = stat_m[h] * c2 + jnp.log2(stat_l[h])
+
+    each_head(finish)
     o_in = [
         remote(o_all.at[pl.ds(two, two)], op.at[0], dev_a),
         remote(o_all.at[pl.ds(row, row)], op.at[1, pl.ds(0, row)], dev_b),
@@ -362,8 +374,10 @@
         add_to(dot_other.at[side[j]], dot_nt(weights(wp, j), both), j in (0, A_CHUNKS))
 
     def send_cotangent(i):
-        for h in range(GROUP):
-            dot_send[i, h] = dot_other[i, h * HD : (h + 1) * HD, :].astype(BF)
+        def low(h):
+            dot_send[i, h] = dot_other[i, span_of(h), :].astype(BF)
+
+        each_head(low)
         return remote(dot_send.at[i], dot_recv.at[i], [dev_a, dev_b][i])
 
     rs = {}
@@ -391,16 +405,16 @@
         )
 
     def turn_own():
-        for h in range(GROUP):
-            turn_d(h, 0, row, dot_own[h * HD : (h + 1) * HD, :].astype(BF))
+        each_head(lambda h: turn_d(h, 0, row, dot_own[span_of(h), :].astype(BF)))
 
     def turn_rest():
-        for h in range(GROUP):
-            at_h = slice(h * HD, (h + 1) * HD)
+        def head(h):
             from_a, from_b = dot_recv[0, h].astype(F32), dot_recv[1, h].astype(F32)
-            turn_d(h, row, row, (dot_part[0, at_h] + from_b[:, 0:row]).astype(BF))
-            turn_d(h, two, row, (dot_part[1, at_h] + from_a[:, 0:row]).astype(BF))
+            turn_d(h, row, row, (dot_part[0, span_of(h)] + from_b[:, 0:row]).astype(BF))
+            turn_d(h, two, row, (dot_part[1, span_of(h)] + from_a[:, 0:row]).astype(BF))
             turn_d(h, 3 * row, row, (from_a[:, row:two] + from_b[:, row:two]).astype(BF))
+
+        each_head(head)
 
     def backward(o, base, size):
         tl = slice(base, base + size)
@@ -512,28 +526,18 @@
     lax.fori_loop(0, REACH - 1, other_rows, 0)
     backward(0, row, tok - row)
 
-    outs = []
-
-    def put(src, dst):
-        c = pltpu.make_async_copy(src, dst, out_sem.at[len(outs)])
-        c.start()
-        outs.append(c)
-
-    for h in range(GROUP):
-        gq_out[:, h * HD : (h + 1) * HD] = (dq_acc[h] * SCALE).T.astype(BF)
-    for s in range(N_TP):
-        rows = pl.ds(pl.multiple_of(perm[s] * row, row), row)
-        put(gq_out.at[pl.ds(s * row, row)], gq_ref.at[rows])
-
+    def put_queries(h):
+        for s in range(N_TP):
+            rows = pl.ds(pl.multiple_of(perm[s] * row, row), row)
+            part = dq_acc[h, :, s * row : (s + 1) * row] * SCALE
+            gq_ref[rows, span_of(h)] = part.T.astype(BF)
+
+    each_head(put_queries)
+    back_copy(1).wait_recv()
+    gk_ref[...], gv_ref[...] = sums(0)
     for j in range(CHUNKS):
         rs[j].wait_recv()
-        lo_out[:, cols[j]] = (lo_acc[:, cols[j]] + rs_recv[:, cols[j]].astype(F32)).astype(BF)
-        put(lo_out.at[:, cols[j]], lo_ref.at[:, cols[j]])
-
-    back_copy(1).wait_recv()
-    gk_out[...], gv_out[...] = sums(0)
-    put(gk_out, gk_ref)
-    put(gv_out, gv_ref)
+        lo_ref[:, cols[j]] = (lo_acc[:, cols[j]] + rs_recv[:, cols[j]].astype(F32)).astype(BF)
 
     sent = [c for pair in kv[1:] for c in pair] + o_in + d_in
     sent += [back_copy(o) for o in range(1, REACH)]
@@ -544,21 +548,14 @@
         sent += [wa[j], up[j], down[j], far[j]] + sibs[j]
     for c in sent:
         c.wait_send()
-    for c in outs:
-        c.wait()
 
 
 def settle(*refs):
-    many = len(refs) // 3
-    came, went, held, sems = refs[:many], refs[many : 2 * many], refs[2 * many : -1], refs[-1]
-    loads = [pltpu.make_async_copy(came[i], held[i], sems.at[0, i]) for i in range(many)]
-    stores = [pltpu.make_async_copy(held[i], went[i], sems.at[1, i]) for i in range(many)]
-    for c in loads:
+    many = len(refs) // 2
+    copies = [pltpu.make_async_copy(refs[i], refs[many + i], refs[-1].at[i]) for i in range(many)]
+    for c in copies:
         c.start()
-    for load, store in zip(loads, stores):
-        load.wait()
-        store.start()
-    for c in stores:
+    for c in copies:
         c.wait()
 
 
@@ -574,13 +571,13 @@
     found = pl.pallas_call(
         functools.partial(kernel, n, docs),
         out_shape=(
-            jax.ShapeDtypeStruct((row, feat), BF),
-            jax.ShapeDtypeStruct((tok, width), BF),
-            jax.ShapeDtypeStruct((tok, HD), BF),
-            jax.ShapeDtypeStruct((tok, HD), BF),
+            vm((row, feat), BF),
+            vm((tok, width), BF),
+            vm((tok, HD), BF),
+            vm((tok, HD), BF),
         ),
         in_specs=[pl.BlockSpec(memory_space=pltpu.SMEM)] + [hbm] * 5,
-        out_specs=(hbm,) * 4,
+        out_specs=(pl.BlockSpec(memory_space=pltpu.VMEM),) * 4,
         scratch_shapes=[
             vm((GROUP, tok, HD), BF),
             vm((GROUP, HD, tok), BF),
@@ -600,7 +597,6 @@
             vm((row, feat), BF),
             vm((row, feat), BF),
             vm((row, feat), F32),
-            vm((row, feat), BF),
             vm((width, row), F32),
             vm((2, width, row), F32),
             vm((2, width, two), F32),
@@ -614,12 +610,8 @@
             vm((GROUP, HD, tok), F32),
             vm((REACH - 1, tok, 2 * HD), BF),
             vm((REACH, tok, 2 * HD), BF),
-            vm((tok, width), BF),
-            vm((tok, HD), BF),
-            vm((tok, HD), BF),
             vm((1, tok), jnp.int32),
             dma((4 + N_TP * GROUP,)),
-            dma((16,)),
             dma((96,)),
             dma((96,)),
         ],
@@ -638,9 +630,9 @@
     return pl.pallas_call(
         settle,
         out_shape=tuple(jax.ShapeDtypeStruct(a.shape, a.dtype) for a in found),
-        in_specs=[hbm] * 4,
+        in_specs=[pl.BlockSpec(memory_space=pltpu.VMEM)] * 4,
         out_specs=(hbm,) * 4,
-        scratch_shapes=[vm(a.shape, a.dtype) for a in found] + [dma((2, 4))],
+        scratch_shapes=[dma((4,))],
     )(*found)
 
 

time: 75.4 us -> 81.4 us (1.080)
  local copies, waits for them, and re-layouts: 0 us -> 3.23 us
  Pallas kernels: 74.5 us -> 77.2 us
    unnamed x0 -> x8, local copies, waits for them, and re-layouts: none -> 3.23 us
    pallas_call x1, Pallas kernels: 71.7 us -> 74.3 us  [on_device(): pl.pallas_call(functools.partial(kernel, n, docs), out_shape=(vm((row, fe...]
where the time goes in v1:
time: 81.4 us; the launch traced here: 81.3 us
  Pallas kernels  77.2 us (95%)
  local copies, waits for them, and re-layouts  3.23 us (4%)
  between operations  0.83 us (1%)
    pallas_call x1, Pallas kernels, on_device(): pl.pallas_call(functools.partial(kernel, n, docs), out_shape=(vm((row, fe...  74.3 us
    unnamed x8, local copies, waits for them, and re-layouts  3.23 us
    pallas_call x1, Pallas kernels, on_device(): pl.pallas_call(settle, out_shape=tuple((jax.ShapeDtypeStruct(a.shape, a.d...  2.91 us

profile of v1, /device:TPU:1, one launch (start us, length us, event | category | flops | bytes accessed | tf_op | source)
XLA Modules:
  0.0 81.3 jit_solution(13863524088479512025)
XLA Ops:
  0.6 74.3 %shard_map.93 = (bf16[128,5120]{1,0:T(8,128)(2,1)S(1)}, bf16[512,640]{1,0:T(8,128)(2,1)S(1)}, bf16[512,128]{1,0:T(8,128)(2,1)S(1)}, bf16[512,128]{1,0:T(8,128)(2,1)S(1)}) custom-call(s32[32]{0:T(128)} %len_ref.1, bf16[512,640]{1,0:T(8,128)(2,1)} %q_ref.1, bf16[512,128]{1,0:T(8,128)(2,1)} %k_ref.1, bf16[512,128]{1,0:T(8,128)(2,1)} %v_ref.1, ...), custom_call_target="tpu_custom_call" | custom-call | flops 16106127360 | bytes 16777216 | tf_op jit(solution)/shard_map/pallas_call | solution.py:571
  74.9 0.0 copy-start
  74.9 1.1 %copy-done = bf16[128,5120]{1,0:T(8,128)(2,1)} copy-done((bf16[128,5120]{1,0:T(8,128)(2,1)}, bf16[128,5120]{1,0:T(8,128)(2,1)S(1)}, u32[]{:S(2)}) %copy-start) | copy-done | bytes 1310744
  76.0 0.0 copy-start.1
  76.0 0.9 %copy-done.1 = bf16[512,640]{1,0:T(8,128)(2,1)} copy-done((bf16[512,640]{1,0:T(8,128)(2,1)}, bf16[512,640]{1,0:T(8,128)(2,1)S(1)}, u32[]{:S(2)}) %copy-start.1) | copy-done | bytes 655384
  76.9 0.0 copy-start.2
  76.9 0.7 copy-done.2
  77.5 0.0 copy-start.3
  77.5 0.7 copy-done.3
  78.2 2.9 %shard_map.94 = (bf16[128,5120]{1,0:T(8,128)(2,1)}, bf16[512,640]{1,0:T(8,128)(2,1)}, bf16[512,128]{1,0:T(8,128)(2,1)}, bf16[512,128]{1,0:T(8,128)(2,1)}) custom-call(bf16[128,5120]{1,0:T(8,128)(2,1)} %copy-done, bf16[512,640]{1,0:T(8,128)(2,1)} %copy-done.1, bf16[512,128]{1,0:T(8,128)(2,1)} %copy-done.2, bf16[512,128]{1,0:T(8,128)(2,1)} %copy-done.3), custom_call_target="tpu_custom_call" | custom-call | tf_op jit(solution)/shard_map/pallas_call | solution.py:630
Async XLA Ops:
  74.9 1.1 %copy-start = (bf16[128,5120]{1,0:T(8,128)(2,1)}, bf16[128,5120]{1,0:T(8,128)(2,1)S(1)}, u32[]{:S(2)}) copy-start(bf16[128,5120]{1,0:T(8,128)(2,1)S(1)} %get-tuple-element.8.refs_0_) | copy-start | bytes 3932164
  76.0 0.9 %copy-start.1 = (bf16[512,640]{1,0:T(8,128)(2,1)}, bf16[512,640]{1,0:T(8,128)(2,1)S(1)}, u32[]{:S(2)}) copy-start(bf16[512,640]{1,0:T(8,128)(2,1)S(1)} %get-tuple-element.9.refs_1_) | copy-start | bytes 1966084
  76.9 0.7 copy-start.2
  77.5 0.7 copy-start.3

commit v2 on v0

--- a/solution.py
+++ b/solution.py
@@ -185,7 +185,6 @@
     ask_rows(1)
     ask_rows(4)
     ask_rows(2)
-    ask_rows(5)
     ask_rows(3)
 
     z_sibs, z_ups, z_downs = [], [], []
@@ -340,6 +339,8 @@
         remote(o_all.at[pl.ds(row, row)], op.at[1, pl.ds(0, row)], dev_b),
         remote(o_all.at[pl.ds(3 * row, row)], op.at[1, pl.ds(row, row)], dev_b),
     ]
+    ask_rows(5)
+
     def weights(w3, j):
         return w3[:, :, cols[j]].reshape(width, wide[j])
 
@@ -447,7 +448,7 @@
         go_in[j].wait_recv()
         cotangent_rows(j)
     z_next(3)
-    for j in (2, 3, 4, 5):
+    for j in (2, 3, 4):
         go_in[j].wait_recv()
         cotangent_rows(j)
     for j in range(A_CHUNKS):
@@ -457,15 +458,18 @@
         have(j)
         cotangent_other(j)
     d_in = [send_cotangent(0)]
+    o_in[0].wait_recv()
+    project(0)
+    send_rows(0)
     for c in z_sibs:
         c.wait_recv()
     cotangent_other(4)
+    go_in[5].wait_recv()
     cotangent_other(5)
     d_in.append(send_cotangent(1))
-    o_in[0].wait_recv()
-    for j in (0, 1):
-        project(j)
-        send_rows(j)
+    project(1)
+    send_rows(1)
+    cotangent_rows(5)
     o_in[1].wait_recv()
     o_in[2].wait_recv()
     for j in (4, 2, 5, 3):

time: 75.4 us -> 79 us (1.048)
  Pallas kernels: 74.5 us -> 78 us
    pallas_call x1, Pallas kernels: 71.7 us -> 75.3 us  [on_device(): pl.pallas_call(functools.partial(kernel, n, docs), out_shape=(jax.ShapeDt...]
where the time goes in v2:
time: 79 us; the launch traced here: 78.8 us
  Pallas kernels  78 us (99%)
  between operations  0.82 us (1%)
    pallas_call x1, Pallas kernels, on_device(): pl.pallas_call(functools.partial(kernel, n, docs), out_shape=(jax.ShapeDt...  75.3 us
    pallas_call x1, Pallas kernels, on_device(): pl.pallas_call(settle, out_shape=tuple((jax.ShapeDtypeStruct(a.shape, a.d...  2.73 us

profile of v2, /device:TPU:1, one launch (start us, length us, event | category | flops | bytes accessed | tf_op | source)
XLA Modules:
  0.0 78.8 jit_solution(6750799559612832888)
XLA Ops:
  0.6 75.3 %shard_map.93 = (bf16[128,5120]{1,0:T(8,128)(2,1)}, bf16[512,640]{1,0:T(8,128)(2,1)}, bf16[512,128]{1,0:T(8,128)(2,1)}, bf16[512,128]{1,0:T(8,128)(2,1)}) custom-call(s32[32]{0:T(128)} %len_ref.1, bf16[512,640]{1,0:T(8,128)(2,1)} %q_ref.1, bf16[512,128]{1,0:T(8,128)(2,1)} %k_ref.1, bf16[512,128]{1,0:T(8,128)(2,1)} %v_ref.1, bf16[8,80,5120]{2,1,0:T(8,128)(2,1)} %bitcast.1, ...), custom_call_target="tpu_custom_call" | custom-call | flops 16106127360 | bytes 16777216 | tf_op jit(solution)/shard_map/pallas_call | solution.py:578
  75.9 2.7 %shard_map.94 = (bf16[128,5120]{1,0:T(8,128)(2,1)}, bf16[512,640]{1,0:T(8,128)(2,1)}, bf16[512,128]{1,0:T(8,128)(2,1)}, bf16[512,128]{1,0:T(8,128)(2,1)}) custom-call(bf16[128,5120]{1,0:T(8,128)(2,1)} %get-tuple-element.8.refs_0_, bf16[512,640]{1,0:T(8,128)(2,1)} %get-tuple-element.9.refs_1_, bf16[512,128]{1,0:T(8,128)(2,1)} %get-tuple-element.10.refs_2_, ...), custom_call_target="tpu_custom_call" | custom-call | tf_op jit(solution)/shard_map/pallas_call | solution.py:642
